TPU v7x, 32 devices: a whole 2x2x4 slice. The times are simulated.
32 devices in a mesh: blk: 16 (over z, y, core), ax: 2 (over x).
Axes of the slice: x: 2, y: 2, z: 4, core: 2. Of those that a mesh axis runs over, the one named last changes fastest.
Arguments:
- pressure_guess: float32 [256, 48, 384], P('blk', 'ax'), may hold values from -6 to 6
- rhs: float32 [256, 48, 384], P('blk', 'ax'), may hold values from -16 to 16
- kappa: float32 [256, 48, 384], P('blk', 'ax'), may hold values from 1.5 to 4
- sigma: float32 [256, 48, 384], P('blk', 'ax'), may hold values from 0.05 to 0.4
Outputs:
- pressure: float32 [256, 48, 384], P('blk', 'ax')
All inputs are finite; a program needn't handle non-finite values.
Results may differ from a plain program's by a relative error of at most 0.00002.
Values sent between devices are 32-bit elements; how exact they have to be, the bound alone decides.
A program may use at most 192 MiB of HBM per device.

v0:
```python
from functools import reduce

import jax
import jax.numpy as jnp
from jax import lax
from jax.sharding import PartitionSpec as P

NU = 2
NC = 4


omega_factor = 0.8


def extended_2(block, sides, width, periodic):
    for axis, dim in sides:
        count = lax.axis_size(axis)
        forward = [(i, i + 1) for i in range(count - 1)]
        if periodic:
            forward.append((count - 1, 0))
        backward = [(target, source) for source, target in forward]
        low = lax.ppermute(
            lax.slice_in_dim(block, block.shape[dim] - width, None, axis=dim), axis, forward
        )
        high = lax.ppermute(lax.slice_in_dim(block, 0, width, axis=dim), axis, backward)
        block = jnp.concatenate([low, block, high], axis=dim)
    return block


def radial_pad(field):
    return jnp.pad(field, ((0, 0), (0, 0), (1, 1)))


def axial_extend(stacked, width):
    return extended_2(stacked, (("ax", 2),), width, False)


def azimuth_extend(field, width):
    return extended_2(field, (("blk", 0),), width, True)


def neighbours(wide):
    count = wide.shape[0]
    rows = wide.shape[1] - 2
    cols = wide.shape[2] - 2

    def cut(shift_a, shift_z, shift_r):
        return wide[
            1 + shift_a : count - 1 + shift_a,
            1 + shift_z : 1 + shift_z + rows,
            1 + shift_r : 1 + shift_r + cols,
        ]

    return (
        cut(0, 0, 0),
        [cut(-1, 0, 0), cut(1, 0, 0), cut(0, -1, 0), cut(0, 1, 0), cut(0, 0, -1), cut(0, 0, 1)],
    )


def level_tables(kappa, sigma, target, width):
    stacked = jnp.stack([kappa, sigma, target])
    wide = extended_2(stacked, (("blk", 1),), width, True)
    wide = axial_extend(wide, width)
    center, near = neighbours(radial_pad(wide[0]))
    faces = [0.5 * (center + other) for other in near]
    diag = reduce(lambda left, right: left + right, faces) + wide[1][1:-1, 1:-1]
    return (faces, diag, wide[2][1:-1, 1:-1], width)


def operate(extended, level):
    faces, diag, target, width = level
    faces = [face for face in faces]
    center, near = neighbours(radial_pad(extended))
    off = reduce(
        lambda left, right: left + right, [face * other for face, other in zip(faces, near)]
    )
    return (center, target - (diag * center - off), diag)


def sweep(extended, level):
    center, resid, diag = operate(extended, level)
    return center + omega_factor * resid / diag


def extended_by(field, width):
    wide = azimuth_extend(field, width)
    return axial_extend(wide[None], width)[0]


def smooth(field, level, count):
    for turn in range(count):
        field = sweep(extended_by(field, 1), level)
    return field


def residual_of(field, level):
    center, resid, diag = operate(extended_by(field, 1), level)
    return resid


def coarsen(field):
    a, z, r = field.shape
    return field.reshape(a // 2, 2, z // 2, 2, r // 2, 2).mean(axis=(1, 3, 5))


def refine(field):
    return jnp.repeat(jnp.repeat(jnp.repeat(field, 2, 0), 2, 1), 2, 2)


def local(pressure_guess, rhs, kappa, sigma):
    width = 1
    level0 = level_tables(kappa, sigma, rhs, width)
    field = smooth(pressure_guess, level0, NU)
    target1 = 4.0 * coarsen(residual_of(field, level0))
    kappa1 = coarsen(kappa)
    sigma1 = 4.0 * coarsen(sigma)
    level1 = level_tables(kappa1, sigma1, target1, width)
    error1 = smooth(jnp.zeros_like(target1), level1, NU)
    target2 = 4.0 * coarsen(residual_of(error1, level1))
    kappa2 = coarsen(kappa1)
    sigma2 = 4.0 * coarsen(sigma1)
    level2 = level_tables(kappa2, sigma2, target2, width)
    error2 = smooth(jnp.zeros_like(target2), level2, NC)
    error1 = smooth(error1 + refine(error2), level1, NU)
    return smooth(field + refine(error1), level0, NU)


def solution(mesh):
    return jax.shard_map(
        local,
        mesh=mesh,
        in_specs=(
            P("blk", "ax", None),
            P("blk", "ax", None),
            P("blk", "ax", None),
            P("blk", "ax", None),
        ),
        out_specs=P("blk", "ax", None),
        check_vma=False,
    )
```

profile of v0, /device:TPU:0, one launch (start us, length us, event | category | flops | bytes accessed | tf_op | source)
XLA Modules:
  0.0 472.7 jit_solution(11327644649587070568)
XLA Ops:
  1.4 5.0 %collective-permute-start.1 = (f32[1,24,384]{2,1,0:T(8,128)S(1)}, f32[1,24,384]{2,1,0:T(8,128)S(1)}, u32[]{:S(2)}, u32[]{:S(2)}) collective-permute-start(f32[1,24,384]{2,1,0:T(8,128)S(1)} %get-tuple-element.52), channel_id=1, source_target_pairs={{2,0},{4,2},{6,4},{8,6},{10,8},{12,10},{14,12},{16,14},{18,16},{20... | collective-permute-start | bytes 110600 | tf_op jit(solution)/shard_map/ppermute | solution.py:25
  7.4 4.4 collective-permute-start.5
  18.3 4.5 collective-permute-start.6
  24.9 4.3 collective-permute-done.7
  32.4 4.4 collective-permute-start.9
  44.1 4.4 collective-permute-start.13
  48.5 40.1 %reshape.92 = f32[8,2,12,2,192,2]{5,4,3,2,1,0:T(8,128)} reshape(f32[16,24,384]{2,1,0:T(8,128)} %param.6) | data formatting | bytes 1179648 | tf_op jit(solution)/shard_map/reshape | solution.py:103
  88.6 40.0 %reshape.93 = f32[8,2,12,2,192,2]{5,4,3,2,1,0:T(8,128)} reshape(f32[16,24,384]{2,1,0:T(8,128)} %param.7) | data formatting | bytes 1179648 | tf_op jit(solution)/shard_map/reshape | solution.py:103
  128.6 14.1 %reduce_sum.54 = f32[8,12,192]{2,1,0:T(8,128)} reduce(f32[8,2,12,2,192,2]{5,4,3,2,1,0:T(8,128)} %reshape.92, f32[]{:T(128)} %constant.12.clone.1), dimensions={1,3,5}, to_apply=%region_0.1 | reduce | flops 129024 | bytes 663556 | tf_op jit(solution)/shard_map/reduce_sum | solution.py:103
  142.8 14.1 %reduce_sum.55 = f32[8,12,192]{2,1,0:T(8,128)} reduce(f32[8,2,12,2,192,2]{5,4,3,2,1,0:T(8,128)} %reshape.93, f32[]{:T(128)} %constant.12.clone.1), dimensions={1,3,5}, to_apply=%region_1.2 | reduce | flops 129024 | bytes 663556 | tf_op jit(solution)/shard_map/reduce_sum | solution.py:103
  160.7 4.4 collective-permute-start.17
  166.8 5.1 %collective-permute-start.18 = (f32[1,18,1,384]{3,2,1,0:T(1,128)S(1)}, f32[1,18,1,384]{3,2,1,0:T(1,128)S(1)}, u32[]{:S(2)}, u32[]{:S(2)}) collective-permute-start(f32[1,18,1,384]{3,2,1,0:T(1,128)S(1)} %get-tuple-element.37), channel_id=1, source_target_pairs={{0,1},{2,3},{4,5},{6,7},{8,9},{10,11},{12,13},{14,15},{16,17},{18,... | collective-permute-start | bytes 82952 | tf_op jit(solution)/shard_map/ppermute | solution.py:22
  179.6 40.0 %reshape.94 = f32[8,2,12,2,192,2]{5,4,3,2,1,0:T(8,128)} reshape(f32[16,24,384]{2,1,0:T(8,128)} %fusion.26) | data formatting | bytes 1179648 | tf_op jit(solution)/shard_map/reshape | solution.py:103
  219.6 14.1 %reduce_sum.56 = f32[8,12,192]{2,1,0:T(8,128)} reduce(f32[8,2,12,2,192,2]{5,4,3,2,1,0:T(8,128)} %reshape.94, f32[]{:T(128)} %constant.12.clone.1), dimensions={1,3,5}, to_apply=%region_2.3 | reduce | flops 129024 | bytes 663556 | tf_op jit(solution)/shard_map/reduce_sum | solution.py:103
  235.5 4.4 collective-permute-start.21
  246.0 4.5 collective-permute-start.22
  259.3 4.4 collective-permute-start.25
  264.4 4.4 collective-permute-start.29
  269.5 7.0 %mul.500 = f32[4,2,6,2,96,2]{5,4,1,0,3,2:T(8,128)} reshape(f32[8,12,192]{2,0,1:T(8,128)} %copy.215) | data formatting | bytes 147456 | tf_op jit(solution)/shard_map/mul | solution.py:116
  287.9 7.0 %div.58 = f32[4,2,6,2,96,2]{5,4,1,0,3,2:T(8,128)} reshape(f32[8,12,192]{2,0,1:T(8,128)} %copy.214) | data formatting | bytes 147456 | tf_op jit(solution)/shard_map/div | solution.py:103
  302.0 4.4 collective-permute-start.33
  307.9 5.1 %collective-permute-start.34 = (f32[1,10,1,192]{3,2,1,0:T(1,128)S(1)}, f32[1,10,1,192]{3,2,1,0:T(1,128)S(1)}, u32[]{:S(2)}, u32[]{:S(2)}) collective-permute-start(f32[1,10,1,192]{3,2,1,0:T(1,128)S(1)} %get-tuple-element.64), channel_id=1, source_target_pairs={{0,1},{2,3},{4,5},{6,7},{8,9},{10,11},{12,13},{14,15},{16,17},{18,... | collective-permute-start | bytes 23048 | tf_op jit(solution)/shard_map/ppermute | solution.py:22
  319.7 7.0 %reshape.95 = f32[4,2,6,2,96,2]{5,4,1,0,3,2:T(8,128)} reshape(f32[8,12,192]{2,0,1:T(8,128)} %copy.219) | data formatting | bytes 147456 | tf_op jit(solution)/shard_map/reshape | solution.py:103
  331.7 4.4 collective-permute-start.37
  340.9 4.5 collective-permute-start.38
  352.0 4.4 collective-permute-start.41
  365.1 4.4 collective-permute-start.45
  378.2 4.4 collective-permute-start.49
  398.9 4.4 collective-permute-start.53
  413.8 4.4 collective-permute-start.57
  442.6 4.4 collective-permute-start.61
  457.3 4.4 collective-permute-start.65
  (306 shorter events, 183.8 us)
Async XLA Ops:
  0.9 10.9 %collective-permute-start = (f32[1,24,384]{2,1,0:T(8,128)S(1)}, f32[1,24,384]{2,1,0:T(8,128)S(1)}, u32[]{:S(2)}, u32[]{:S(2)}) collective-permute-start(f32[1,24,384]{2,1,0:T(8,128)S(1)} %get-tuple-element.51), channel_id=1, source_target_pairs={{0,2},{2,4},{4,6},{6,8},{8,10},{10,12},{12,14},{14,16},{16,18},{18... | collective-permute-start | bytes 110600 | tf_op jit(solution)/shard_map/ppermute | solution.py:22
  1.4 10.4 %collective-permute-start.1 = (f32[1,24,384]{2,1,0:T(8,128)S(1)}, f32[1,24,384]{2,1,0:T(8,128)S(1)}, u32[]{:S(2)}, u32[]{:S(2)}) collective-permute-start(f32[1,24,384]{2,1,0:T(8,128)S(1)} %get-tuple-element.52), channel_id=1, source_target_pairs={{2,0},{4,2},{6,4},{8,6},{10,8},{12,10},{14,12},{16,14},{18,16},{20... | collective-permute-start | bytes 110600 | tf_op jit(solution)/shard_map/ppermute | solution.py:25
  7.3 10.8 %collective-permute-start.4 = (f32[3,1,24,384]{3,2,1,0:T(8,128)S(1)}, f32[3,1,24,384]{3,2,1,0:T(8,128)S(1)}, u32[]{:S(2)}, u32[]{:S(2)}) collective-permute-start(f32[3,1,24,384]{3,2,1,0:T(8,128)S(1)} %get-tuple-element.31), channel_id=1, source_target_pairs={{0,2},{2,4},{4,6},{6,8},{8,10},{10,12},{12,14},{14,16},{16,18},{18... | collective-permute-start | bytes 331784 | tf_op jit(solution)/shard_map/ppermute | solution.py:22
  7.4 10.7 %collective-permute-start.5 = (f32[3,1,24,384]{3,2,1,0:T(8,128)S(1)}, f32[3,1,24,384]{3,2,1,0:T(8,128)S(1)}, u32[]{:S(2)}, u32[]{:S(2)}) collective-permute-start(f32[3,1,24,384]{3,2,1,0:T(8,128)S(1)} %get-tuple-element.32), channel_id=1, source_target_pairs={{2,0},{4,2},{6,4},{8,6},{10,8},{12,10},{14,12},{16,14},{18,16},{20... | collective-permute-start | bytes 331784 | tf_op jit(solution)/shard_map/ppermute | solution.py:25
  13.0 11.1 %collective-permute-start.2 = (f32[1,18,1,384]{3,2,1,0:T(1,128)S(1)}, f32[1,18,1,384]{3,2,1,0:T(1,128)S(1)}, u32[]{:S(2)}, u32[]{:S(2)}) collective-permute-start(f32[1,18,1,384]{3,2,1,0:T(1,128)S(1)} %get-tuple-element.41), channel_id=1, source_target_pairs={{0,1},{2,3},{4,5},{6,7},{8,9},{10,11},{12,13},{14,15},{16,17},{18,... | collective-permute-start | bytes 82952 | tf_op jit(solution)/shard_map/ppermute | solution.py:22
  16.8 7.4 %collective-permute-start.3 = (f32[1,18,1,384]{3,2,1,0:T(1,128)S(1)}, f32[1,18,1,384]{3,2,1,0:T(1,128)S(1)}, u32[]{:S(2)}, u32[]{:S(2)}) collective-permute-start(f32[1,18,1,384]{3,2,1,0:T(1,128)S(1)} %get-tuple-element.42), channel_id=1, source_target_pairs={{1,0},{3,2},{5,4},{7,6},{9,8},{11,10},{13,12},{15,14},{17,16},{19,... | collective-permute-start | bytes 82952 | tf_op jit(solution)/shard_map/ppermute | solution.py:25
  18.3 6.6 %collective-permute-start.6 = (f32[3,18,1,384]{3,2,1,0:T(1,128)S(1)}, f32[3,18,1,384]{3,2,1,0:T(1,128)S(1)}, u32[]{:S(2)}, u32[]{:S(2)}) collective-permute-start(f32[3,18,1,384]{3,2,1,0:T(1,128)S(1)} %get-tuple-element.29), channel_id=1, source_target_pairs={{0,1},{2,3},{4,5},{6,7},{8,9},{10,11},{12,13},{14,15},{16,17},{18,... | collective-permute-start | bytes 248840 | tf_op jit(solution)/shard_map/ppermute | solution.py:22
  22.8 6.3 %collective-permute-start.7 = (f32[3,18,1,384]{3,2,1,0:T(1,128)S(1)}, f32[3,18,1,384]{3,2,1,0:T(1,128)S(1)}, u32[]{:S(2)}, u32[]{:S(2)}) collective-permute-start(f32[3,18,1,384]{3,2,1,0:T(1,128)S(1)} %get-tuple-element.30), channel_id=1, source_target_pairs={{1,0},{3,2},{5,4},{7,6},{9,8},{11,10},{13,12},{15,14},{17,16},{19,... | collective-permute-start | bytes 248840 | tf_op jit(solution)/shard_map/ppermute | solution.py:25
  40.0 116.9 %collective-permute-start.10 = (f32[1,18,1,384]{3,2,1,0:T(1,128)}, f32[1,18,1,384]{3,2,1,0:T(1,128)}, u32[]{:S(2)}, u32[]{:S(2)}) collective-permute-start(f32[1,18,1,384]{3,2,1,0:T(1,128)} %get-tuple-element.39), channel_id=1, source_target_pairs={{0,1},{2,3},{4,5},{6,7},{8,9},{10,11},{12,13},{14,15},{16,17},{18,... | collective-permute-start | bytes 82952 | tf_op jit(solution)/shard_map/ppermute | solution.py:22
  42.2 114.7 %collective-permute-start.11 = (f32[1,18,1,384]{3,2,1,0:T(1,128)}, f32[1,18,1,384]{3,2,1,0:T(1,128)}, u32[]{:S(2)}, u32[]{:S(2)}) collective-permute-start(f32[1,18,1,384]{3,2,1,0:T(1,128)} %get-tuple-element.40), channel_id=1, source_target_pairs={{1,0},{3,2},{5,4},{7,6},{9,8},{11,10},{13,12},{15,14},{17,16},{19,... | collective-permute-start | bytes 82952 | tf_op jit(solution)/shard_map/ppermute | solution.py:25
  44.1 129.4 %collective-permute-start.12 = (f32[1,12,192]{2,1,0:T(8,128)}, f32[1,12,192]{2,1,0:T(8,128)S(1)}, u32[]{:S(2)}, u32[]{:S(2)}) collective-permute-start(f32[1,12,192]{2,1,0:T(8,128)} %broadcast.132), channel_id=1, source_target_pairs={{0,2},{2,4},{4,6},{6,8},{8,10},{10,12},{12,14},{14,16},{16,18},{18... | collective-permute-start | bytes 27656 | tf_op jit(solution)/shard_map/ppermute | solution.py:22
  44.1 129.4 %collective-permute-start.13 = (f32[1,12,192]{2,1,0:T(8,128)}, f32[1,12,192]{2,1,0:T(8,128)}, u32[]{:S(2)}, u32[]{:S(2)}) collective-permute-start(f32[1,12,192]{2,1,0:T(8,128)} %broadcast.132), channel_id=1, source_target_pairs={{2,0},{4,2},{6,4},{8,6},{10,8},{12,10},{14,12},{16,14},{18,16},{20... | collective-permute-start | bytes 27656 | tf_op jit(solution)/shard_map/ppermute | solution.py:25
  160.6 6.1 %collective-permute-start.16 = (f32[1,24,384]{2,1,0:T(8,128)S(1)}, f32[1,24,384]{2,1,0:T(8,128)S(1)}, u32[]{:S(2)}, u32[]{:S(2)}) collective-permute-start(f32[1,24,384]{2,1,0:T(8,128)S(1)} %get-tuple-element.47), channel_id=1, source_target_pairs={{0,2},{2,4},{4,6},{6,8},{8,10},{10,12},{12,14},{14,16},{16,18},{18... | collective-permute-start | bytes 110600 | tf_op jit(solution)/shard_map/ppermute | solution.py:22
  166.8 8.1 %collective-permute-start.18 = (f32[1,18,1,384]{3,2,1,0:T(1,128)S(1)}, f32[1,18,1,384]{3,2,1,0:T(1,128)S(1)}, u32[]{:S(2)}, u32[]{:S(2)}) collective-permute-start(f32[1,18,1,384]{3,2,1,0:T(1,128)S(1)} %get-tuple-element.37), channel_id=1, source_target_pairs={{0,1},{2,3},{4,5},{6,7},{8,9},{10,11},{12,13},{14,15},{16,17},{18,... | collective-permute-start | bytes 82952 | tf_op jit(solution)/shard_map/ppermute | solution.py:22
  235.4 9.6 %collective-permute-start.20 = (f32[3,1,12,192]{3,2,1,0:T(8,128)S(1)}, f32[3,1,12,192]{3,2,1,0:T(8,128)S(1)}, u32[]{:S(2)}, u32[]{:S(2)}) collective-permute-start(f32[3,1,12,192]{3,2,1,0:T(8,128)S(1)} %get-tuple-element.58), channel_id=1, source_target_pairs={{0,2},{2,4},{4,6},{6,8},{8,10},{10,12},{12,14},{14,16},{16,18},{18... | collective-permute-start | bytes 82952 | tf_op jit(solution)/shard_map/ppermute | solution.py:22
  235.5 9.5 %collective-permute-start.21 = (f32[3,1,12,192]{3,2,1,0:T(8,128)S(1)}, f32[3,1,12,192]{3,2,1,0:T(8,128)S(1)}, u32[]{:S(2)}, u32[]{:S(2)}) collective-permute-start(f32[3,1,12,192]{3,2,1,0:T(8,128)S(1)} %get-tuple-element.59), channel_id=1, source_target_pairs={{2,0},{4,2},{6,4},{8,6},{10,8},{12,10},{14,12},{16,14},{18,16},{20... | collective-permute-start | bytes 82952 | tf_op jit(solution)/shard_map/ppermute | solution.py:25
  241.9 9.9 %collective-permute-start.14 = (f32[1,10,1,192]{3,2,1,0:T(1,128)S(1)}, f32[1,10,1,192]{3,2,1,0:T(1,128)S(1)}, u32[]{:S(2)}, u32[]{:S(2)}) collective-permute-start(f32[1,10,1,192]{3,2,1,0:T(1,128)S(1)} %get-tuple-element.68), channel_id=1, source_target_pairs={{0,1},{2,3},{4,5},{6,7},{8,9},{10,11},{12,13},{14,15},{16,17},{18,... | collective-permute-start | bytes 23048 | tf_op jit(solution)/shard_map/ppermute | solution.py:22
  243.7 8.2 %collective-permute-start.15 = (f32[1,10,1,192]{3,2,1,0:T(1,128)S(1)}, f32[1,10,1,192]{3,2,1,0:T(1,128)S(1)}, u32[]{:S(2)}, u32[]{:S(2)}) collective-permute-start(f32[1,10,1,192]{3,2,1,0:T(1,128)S(1)} %get-tuple-element.69), channel_id=1, source_target_pairs={{1,0},{3,2},{5,4},{7,6},{9,8},{11,10},{13,12},{15,14},{17,16},{19,... | collective-permute-start | bytes 23048 | tf_op jit(solution)/shard_map/ppermute | solution.py:25
  259.3 20.6 %collective-permute-start.24 = (f32[1,12,192]{2,1,0:T(8,128)}, f32[1,12,192]{2,1,0:T(8,128)S(1)}, u32[]{:S(2)}, u32[]{:S(2)}) collective-permute-start(f32[1,12,192]{2,1,0:T(8,128)} %get-tuple-element.80), channel_id=1, source_target_pairs={{0,2},{2,4},{4,6},{6,8},{8,10},{10,12},{12,14},{14,16},{16,18},{18... | collective-permute-start | bytes 27656 | tf_op jit(solution)/shard_map/ppermute | solution.py:22
  259.3 20.6 %collective-permute-start.25 = (f32[1,12,192]{2,1,0:T(8,128)}, f32[1,12,192]{2,1,0:T(8,128)}, u32[]{:S(2)}, u32[]{:S(2)}) collective-permute-start(f32[1,12,192]{2,1,0:T(8,128)} %get-tuple-element.81), channel_id=1, source_target_pairs={{2,0},{4,2},{6,4},{8,6},{10,8},{12,10},{14,12},{16,14},{18,16},{20... | collective-permute-start | bytes 27656 | tf_op jit(solution)/shard_map/ppermute | solution.py:25
  264.4 50.2 %collective-permute-start.28 = (f32[1,6,96]{2,0,1:T(1,128)}, f32[1,6,96]{2,0,1:T(1,128)}, u32[]{:S(2)}, u32[]{:S(2)}) collective-permute-start(f32[1,6,96]{2,0,1:T(1,128)} %broadcast.135), channel_id=1, source_target_pairs={{0,2},{2,4},{4,6},{6,8},{8,10},{10,12},{12,14},{14,16},{16,18},{18... | collective-permute-start | bytes 6920 | tf_op jit(solution)/shard_map/ppermute | solution.py:22
  264.4 50.2 %collective-permute-start.29 = (f32[1,6,96]{2,0,1:T(1,128)}, f32[1,6,96]{2,0,1:T(1,128)}, u32[]{:S(2)}, u32[]{:S(2)}) collective-permute-start(f32[1,6,96]{2,0,1:T(1,128)} %broadcast.135), channel_id=1, source_target_pairs={{2,0},{4,2},{6,4},{8,6},{10,8},{12,10},{14,12},{16,14},{18,16},{20... | collective-permute-start | bytes 6920 | tf_op jit(solution)/shard_map/ppermute | solution.py:25
  282.1 17.4 %collective-permute-start.26 = (f32[1,10,1,192]{3,2,1,0:T(1,128)}, f32[1,10,1,192]{3,2,1,0:T(1,128)}, u32[]{:S(2)}, u32[]{:S(2)}) collective-permute-start(f32[1,10,1,192]{3,2,1,0:T(1,128)} %get-tuple-element.66), channel_id=1, source_target_pairs={{0,1},{2,3},{4,5},{6,7},{8,9},{10,11},{12,13},{14,15},{16,17},{18,... | collective-permute-start | bytes 23048 | tf_op jit(solution)/shard_map/ppermute | solution.py:22
  284.3 15.2 %collective-permute-start.27 = (f32[1,10,1,192]{3,2,1,0:T(1,128)}, f32[1,10,1,192]{3,2,1,0:T(1,128)}, u32[]{:S(2)}, u32[]{:S(2)}) collective-permute-start(f32[1,10,1,192]{3,2,1,0:T(1,128)} %get-tuple-element.67), channel_id=1, source_target_pairs={{1,0},{3,2},{5,4},{7,6},{9,8},{11,10},{13,12},{15,14},{17,16},{19,... | collective-permute-start | bytes 23048 | tf_op jit(solution)/shard_map/ppermute | solution.py:25
  307.9 8.2 %collective-permute-start.34 = (f32[1,10,1,192]{3,2,1,0:T(1,128)S(1)}, f32[1,10,1,192]{3,2,1,0:T(1,128)S(1)}, u32[]{:S(2)}, u32[]{:S(2)}) collective-permute-start(f32[1,10,1,192]{3,2,1,0:T(1,128)S(1)} %get-tuple-element.64), channel_id=1, source_target_pairs={{0,1},{2,3},{4,5},{6,7},{8,9},{10,11},{12,13},{14,15},{16,17},{18,... | collective-permute-start | bytes 23048 | tf_op jit(solution)/shard_map/ppermute | solution.py:22
  331.6 8.5 %collective-permute-start.36 = (f32[3,1,6,96]{3,1,2,0:T(1,128)S(1)}, f32[3,1,6,96]{3,1,2,0:T(1,128)S(1)}, u32[]{:S(2)}, u32[]{:S(2)}) collective-permute-start(f32[3,1,6,96]{3,1,2,0:T(1,128)S(1)} %get-tuple-element.87), channel_id=1, source_target_pairs={{0,2},{2,4},{4,6},{6,8},{8,10},{10,12},{12,14},{14,16},{16,18},{18... | collective-permute-start | bytes 20744 | tf_op jit(solution)/shard_map/ppermute | solution.py:22
  331.7 8.5 %collective-permute-start.37 = (f32[3,1,6,96]{3,1,2,0:T(1,128)S(1)}, f32[3,1,6,96]{3,1,2,0:T(1,128)S(1)}, u32[]{:S(2)}, u32[]{:S(2)}) collective-permute-start(f32[3,1,6,96]{3,1,2,0:T(1,128)S(1)} %get-tuple-element.88), channel_id=1, source_target_pairs={{2,0},{4,2},{6,4},{8,6},{10,8},{12,10},{14,12},{16,14},{18,16},{20... | collective-permute-start | bytes 20744 | tf_op jit(solution)/shard_map/ppermute | solution.py:25
  336.8 9.9 %collective-permute-start.30 = (f32[1,6,1,96]{3,1,2,0:T(8,128)S(1)}, f32[1,6,1,96]{3,1,2,0:T(8,128)S(1)}, u32[]{:S(2)}, u32[]{:S(2)}) collective-permute-start(f32[1,6,1,96]{3,1,2,0:T(8,128)S(1)} %get-tuple-element.95), channel_id=1, source_target_pairs={{0,1},{2,3},{4,5},{6,7},{8,9},{10,11},{12,13},{14,15},{16,17},{18,... | collective-permute-start | bytes 6920 | tf_op jit(solution)/shard_map/ppermute | solution.py:22
  338.9 7.9 %collective-permute-start.31 = (f32[1,6,1,96]{3,1,2,0:T(8,128)S(1)}, f32[1,6,1,96]{3,1,2,0:T(8,128)S(1)}, u32[]{:S(2)}, u32[]{:S(2)}) collective-permute-start(f32[1,6,1,96]{3,1,2,0:T(8,128)S(1)} %get-tuple-element.96), channel_id=1, source_target_pairs={{1,0},{3,2},{5,4},{7,6},{9,8},{11,10},{13,12},{15,14},{17,16},{19,... | collective-permute-start | bytes 6920 | tf_op jit(solution)/shard_map/ppermute | solution.py:25
  340.9 6.6 %collective-permute-start.38 = (f32[3,6,1,96]{3,1,2,0:T(8,128)S(1)}, f32[3,6,1,96]{3,1,2,0:T(8,128)S(1)}, u32[]{:S(2)}, u32[]{:S(2)}) collective-permute-start(f32[3,6,1,96]{3,1,2,0:T(8,128)S(1)} %get-tuple-element.85), channel_id=1, source_target_pairs={{0,1},{2,3},{4,5},{6,7},{8,9},{10,11},{12,13},{14,15},{16,17},{18,... | collective-permute-start | bytes 20744 | tf_op jit(solution)/shard_map/ppermute | solution.py:22
  442.5 6.1 %collective-permute-start.60 = (f32[1,24,384]{2,1,0:T(8,128)S(1)}, f32[1,24,384]{2,1,0:T(8,128)S(1)}, u32[]{:S(2)}, u32[]{:S(2)}) collective-permute-start(f32[1,24,384]{2,1,0:T(8,128)S(1)} %get-tuple-element.45), channel_id=1, source_target_pairs={{0,2},{2,4},{4,6},{6,8},{8,10},{10,12},{12,14},{14,16},{16,18},{18... | collective-permute-start | bytes 110600 | tf_op jit(solution)/shard_map/ppermute | solution.py:22
  457.3 6.1 %collective-permute-start.64 = (f32[1,24,384]{2,1,0:T(8,128)S(1)}, f32[1,24,384]{2,1,0:T(8,128)S(1)}, u32[]{:S(2)}, u32[]{:S(2)}) collective-permute-start(f32[1,24,384]{2,1,0:T(8,128)S(1)} %get-tuple-element.43), channel_id=1, source_target_pairs={{0,2},{2,4},{4,6},{6,8},{8,10},{10,12},{12,14},{14,16},{16,18},{18... | collective-permute-start | bytes 110600 | tf_op jit(solution)/shard_map/ppermute | solution.py:22
  (72 other events, 815.6 us)
where the time goes:
time: 475 us; the launch traced here: 473 us
  local copies, waits for them, and re-layouts  175 us (37%)
  starting transfers between devices  147 us (31%)
  other arithmetic  88.7 us (19%)
  waiting for transfers between devices  61.1 us (13%)
    reshape x4, local copies, waits for them, and re-layouts, coarsen(): return field.reshape(a // 2, 2, z // 2, 2, r // 2, 2).mean(axis=(1, 3, 5))  127 us
    ppermute x34, starting transfers between devices, extended_2(): lax.ppermute(lax.slice_in_dim(block, 0, width, axis=dim), axis, backward)  98.3 us
    reduce_sum x6, other arithmetic, coarsen(): return field.reshape(a // 2, 2, z // 2, 2, r // 2, 2).mean(axis=(1, 3, 5))  52.7 us
    ppermute x34, starting transfers between devices, extended_2(): lax.ppermute(lax.slice_in_dim(block, block.shape[dim] - width, None, axis...  48.5 us
    ppermute x34, waiting for transfers between devices, extended_2(): lax.ppermute(lax.slice_in_dim(block, 0, width, axis=dim), axis, backward)  46.9 us
    ppermute x34, waiting for transfers between devices, extended_2(): lax.ppermute(lax.slice_in_dim(block, block.shape[dim] - width, None, axis...  14.2 us
    add x12, other arithmetic, sweep(): return center + omega_factor * resid / diag  12.4 us
    reshape x5, local copies, waits for them, and re-layouts, refine(): return jnp.repeat(jnp.repeat(jnp.repeat(field, 2, 0), 2, 1), 2, 2)  11.6 us
  transfers between devices with their start and end apart: 68, of which 26 were waited for; matrix products, arithmetic and copies ran while one was open for 33% of the time, Pallas kernels for 0%

commit v1 on v0

v1 whole, which is shorter than its diff:
```python
import functools

import jax
import jax.numpy as jnp
import numpy as np
from jax import lax
from jax.experimental import pallas as pl
from jax.experimental.pallas import tpu as pltpu
from jax.sharding import PartitionSpec as P

OMEGA = 0.8
F32 = jnp.float32
BF16 = jnp.bfloat16


def up8(count):
    return -(-count // 8) * 8


def pad128(count):
    return -(-count // 128) * 128


class Level:
    def __init__(self, layers, rows, cols, halo):
        self.layers, self.rows, self.cols, self.halo = layers, rows, cols, halo
        self.lanes = pad128(cols)
        self.send_rows = up8(rows)
        self.ring = up8(rows + 2 * halo)
        self.deep = layers + 2 * halo

    def shape(self):
        return (self.deep, self.ring, self.lanes)


class Exchange:
    def __init__(self, level, widths, staged):
        self.level, self.widths, self.staged = level, widths, staged
        wide = max(widths.values())
        steps = range(1, -(-wide // level.layers) + 1)
        self.das = [s * d for d in steps for s in (1, -1)]
        self.blocks = []
        for da in self.das:
            for name, w in widths.items():
                c = min(w - (abs(da) - 1) * level.layers, level.layers)
                if c > 0:
                    base = (abs(da) - 1) * level.layers
                    if da > 0:
                        self.blocks.append((da, name, c, level.layers - c, -base - c))
                    else:
                        self.blocks.append((da, name, c, 0, level.layers + base))
        self.packs = []
        for dz in (1, -1):
            for da in [0] + self.das:
                pairs = []
                for name, w in widths.items():
                    for layer in range(level.layers):
                        if da > 0:
                            far, there = level.layers * da - layer, layer - level.layers * da
                        elif da < 0:
                            far, there = layer + 1 - level.layers * (da + 1), layer - level.layers * da
                        else:
                            far, there = 0, layer
                        for i in range(w - far):
                            if i >= level.rows:
                                continue
                            if dz > 0:
                                here_row, there_row = level.rows - 1 - i, level.ring - 1 - i
                            else:
                                here_row, there_row = i, level.rows + i
                            pairs.append((name, layer, here_row, there + level.halo, there_row))
                if pairs:
                    self.packs.append((da, dz, pairs))

    def count(self):
        return len(self.blocks) + len(self.packs)


def plan(layers, rows, cols):
    lv = [
        Level(layers, rows, cols, 2),
        Level(layers // 2, rows // 2, cols // 2, 5),
        Level(layers // 4, rows // 4, cols // 4, 6),
    ]
    ex = {
        "r1": Exchange(lv[0], {"k0": 2, "ua": 1, "s0": 1, "f0": 1}, False),
        "r2": Exchange(lv[0], {"ub": 1}, False),
        "r3": Exchange(lv[0], {"uc": 2}, False),
        "t1": Exchange(lv[1], {"k1": 5, "s1": 4}, True),
        "t2": Exchange(lv[2], {"k2": 6, "s2": 5}, True),
        "f1": Exchange(lv[1], {"f1": 4}, True),
        "f2": Exchange(lv[2], {"f2": 5}, True),
    }
    scratch = {}
    for name in ("k0", "s0", "f0", "ua", "ub", "uc", "ud", "ue", "ca0", "cz0", "cr0", "d0", "w0"):
        scratch[name] = pltpu.VMEM(lv[0].shape(), F32)
    for i in (1, 2):
        for name in ("k", "s", "f", "ca", "cz", "cr", "d", "w", "ea", "eb", "ec", "ed"):
            scratch[name + str(i)] = pltpu.VMEM(lv[i].shape(), F32)
        for name in ("k", "s", "f"):
            scratch["x" + name + str(i)] = pltpu.VMEM((lv[i].layers, lv[i].send_rows, lv[i].lanes), F32)
    scratch["res0"] = pltpu.VMEM((lv[0].layers, lv[0].send_rows, lv[0].lanes), F32)
    scratch["res1"] = pltpu.VMEM((lv[1].layers, lv[1].send_rows, lv[1].lanes), F32)
    total = 0
    for key, e in ex.items():
        e.key, e.first = key, total
        total += e.count()
        if e.staged:
            for b, (da, name, c, src, dst) in enumerate(e.blocks):
                scratch[f"{key}_b{b}"] = pltpu.VMEM((c, e.level.send_rows, e.level.lanes), F32)
        for p, (da, dz, pairs) in enumerate(e.packs):
            for side in "sr":
                scratch[f"{key}_{side}{p}"] = pltpu.VMEM((up8(len(pairs)), e.level.lanes), F32)
    scratch["ssem"] = pltpu.SemaphoreType.DMA((total,))
    scratch["rsem"] = pltpu.SemaphoreType.DMA((total,))
    scratch["lsem"] = pltpu.SemaphoreType.DMA((4,))
    return lv, ex, scratch


def halve_cols(fine, coarse):
    return (np.arange(fine.lanes)[:, None] // 2 == np.arange(coarse.lanes)[None, :]) & (
        np.arange(coarse.lanes)[None, :] < coarse.cols
    )


def halve_rows(fine, coarse):
    one = (np.arange(fine.send_rows)[None, :] // 2 == np.arange(coarse.send_rows)[:, None]) & (
        np.arange(fine.send_rows)[None, :] < fine.rows
    )
    return np.kron(np.eye(coarse.layers), one)


def double_rows(fine, coarse, count, width):
    one = np.zeros((fine.ring, coarse.ring))
    for z in range(-width, fine.rows + width):
        one[z % fine.ring, (z // 2) % coarse.ring] = 1.0
    return np.kron(np.eye(count), one)


def pieces(value):
    high = value.astype(BF16)
    rest = value - high.astype(F32)
    mid = rest.astype(BF16)
    low = (rest - mid.astype(F32)).astype(BF16)
    return high, mid, low


def right(value, matrix):
    return sum(jnp.dot(part, matrix, preferred_element_type=F32) for part in pieces(value))


def left(matrix, value):
    return sum(jnp.dot(matrix, part, preferred_element_type=F32) for part in pieces(value))


def kernel(lv, ex, names, nblk, nax, *refs):
    (g_in, f_in, k_in, s_in, c0, c1, h0, h1, b0, b1, d0, d1, out) = refs[:13]
    v = dict(zip(names, refs[13:]))
    blk, ax = lax.axis_index("blk"), lax.axis_index("ax")
    has = {1: ax < nax - 1, -1: ax > 0}

    def device(da, dz):
        return {"blk": lax.rem(blk + da + nblk, nblk), "ax": ax + dz}

    def when(dz, work):
        if dz == 0:
            work()
        else:
            pl.when(has[dz])(work)

    local = []
    for i, (src, name) in enumerate(((k_in, "k0"), (g_in, "ua"), (s_in, "s0"), (f_in, "f0"))):
        l0 = lv[0]
        local.append(
            pltpu.make_async_copy(
                src, v[name].at[pl.ds(l0.halo, l0.layers), pl.ds(0, l0.rows), :], v["lsem"].at[i]
            )
        )
        local[-1].start()

    l0 = lv[0]
    pad = (l0.deep, l0.ring - l0.rows, l0.lanes)
    for name in ("k0", "s0", "f0", "ua", "ub", "uc"):
        v[name][:, l0.rows : l0.ring, :] = jnp.zeros(pad, F32)
    for i in (1, 2):
        for name in ("k", "s", "f"):
            v[name + str(i)][...] = jnp.zeros(lv[i].shape(), F32)

    far = range(-2, 3)
    barrier = pltpu.get_barrier_semaphore()
    for dz in (0, 1, -1):
        def greet(dz=dz):
            for da in far:
                if (da, dz) != (0, 0):
                    pl.semaphore_signal(barrier, inc=1, device_id=device(da, dz))
        when(dz, greet)
    for copy in local:
        copy.wait()

    def messages(e):
        m = e.first
        for b, (da, name, c, src, dst) in enumerate(e.blocks):
            lev = e.level
            if e.staged:
                source, target = v["x" + name].at[pl.ds(src, c)], v[f"{e.key}_b{b}"]
            else:
                source = v[name].at[pl.ds(src + lev.halo, c), pl.ds(0, lev.rows), :]
                target = v[name].at[pl.ds(dst + lev.halo, c), pl.ds(0, lev.rows), :]
            yield da, 0, source, target, m, None, None
            m += 1
        for p, (da, dz, pairs) in enumerate(e.packs):
            yield da, dz, v[f"{e.key}_s{p}"], v[f"{e.key}_r{p}"], m, p, pairs
            m += 1

    def descriptor(message):
        da, dz, source, target, m, p, pairs = message
        return pltpu.make_async_remote_copy(
            source, target, v["ssem"].at[m], v["rsem"].at[m], device_id=device(da, dz)
        )

    def pack(e):
        for dz in (1, -1):
            def work(dz=dz):
                for da, dz_, source, target, m, p, pairs in messages(e):
                    if dz_ == dz:
                        for i, (name, layer, row, l_, r_) in enumerate(pairs):
                            if e.staged:
                                line = v["x" + name][layer, row : row + 1, :]
                            else:
                                line = v[name][layer + e.level.halo, row : row + 1, :]
                            source[i : i + 1, :] = line
            when(dz, work)

    def send(e):
        for dz in (1, -1, 0):
            def work(dz=dz):
                for message in messages(e):
                    if message[1] == dz:
                        descriptor(message).start()
            when(dz, work)

    def receive(e):
        for message in messages(e):
            if message[1] == 0:
                descriptor(message).wait_recv()
        if e.staged:
            lev = e.level
            for name in e.widths:
                v[name][lev.halo : lev.halo + lev.layers, 0 : lev.send_rows, :] = v["x" + name][...]
            for b, (da, name, c, src, dst) in enumerate(e.blocks):
                v[name][dst + lev.halo : dst + lev.halo + c, 0 : lev.send_rows, :] = v[f"{e.key}_b{b}"][...]
        for dz in (1, -1):
            def work(dz=dz):
                for message in messages(e):
                    if message[1] == dz:
                        descriptor(message).wait_recv()
                        for i, (name, l_, r_, layer, row) in enumerate(message[6]):
                            v[name][layer, row : row + 1, :] = message[3][i : i + 1, :]
            when(-dz, work)

    def sent(e):
        for dz in (0, 1, -1):
            def work(dz=dz):
                for message in messages(e):
                    if message[1] == dz:
                        descriptor(message).wait_send()
            when(dz, work)

    def loop(first, last, body):
        def step(i, carry):
            body(i)
            return carry
        lax.fori_loop(first, last, step, 0)

    def tables(i, width):
        lev = lv[i]
        k, s, ca, cz, cr, d, w = (v[n + str(i)] for n in ("k", "s", "ca", "cz", "cr", "d", "w"))
        lane = lax.broadcasted_iota(jnp.int32, (lev.ring, lev.lanes), 1)

        def body(l):
            mid, prev, after = k[l], k[l - 1], k[l + 1]
            up = pltpu.roll(mid, lev.ring - 1, 0)
            down = pltpu.roll(mid, 1, 0)
            inner = jnp.where(lane == lev.cols - 1, 0.0, pltpu.roll(mid, lev.lanes - 1, 1))
            outer = jnp.where(lane == 0, 0.0, pltpu.roll(mid, 1, 1))
            ca[l] = 0.5 * (mid + after)
            cz[l] = 0.5 * (mid + up)
            cr[l] = jnp.where(lane == lev.cols - 1, 0.0, 0.5 * (mid + inner))
            diag = 3.0 * mid + 0.5 * (((prev + after) + (up + down)) + (inner + outer)) + s[l]
            d[l] = diag
            w[l] = jnp.where(mid > 0.0, OMEGA / diag, 0.0)

        begin, end = lev.halo - width, lev.halo + lev.layers + width
        ca[begin - 1] = 0.5 * (k[begin - 1] + k[begin])
        loop(begin, end, body)

    def residual(i, u, l):
        lev = lv[i]
        f, ca, cz, cr, d = (v[n + str(i)] for n in ("f", "ca", "cz", "cr", "d"))
        mid = u[l]
        z, r = cz[l], cr[l]
        off = ca[l] * u[l + 1] + ca[l - 1] * u[l - 1]
        off += z * pltpu.roll(mid, lev.ring - 1, 0) + pltpu.roll(z * mid, 1, 0)
        off += r * pltpu.roll(mid, lev.lanes - 1, 1) + pltpu.roll(r * mid, 1, 1)
        return mid, f[l] - (d[l] * mid - off)

    def sweep(i, u, new, width):
        lev = lv[i]
        rows = lev.ring if width else lev.send_rows

        def body(l):
            mid, res = residual(i, u, l)
            value = mid + v["w" + str(i)][l] * res
            new[l, 0:rows, :] = value[0:rows]

        loop(lev.halo - width, lev.halo + lev.layers + width, body)

    def restrict(i, source, target, scale):
        fine, coarse = lv[i], lv[i + 1]
        value = source[...].reshape(coarse.layers, 2, fine.send_rows, fine.lanes)
        value = (value[:, 0] + value[:, 1]) * scale
        value = value.reshape(coarse.layers * fine.send_rows, fine.lanes)
        value = left((h0, h1)[i][...], right(value, (c0, c1)[i][...]))
        target[...] = value.reshape(coarse.layers, coarse.send_rows, coarse.lanes)

    def add_prolonged(i, base, error, new, width):
        fine, coarse = lv[i], lv[i + 1]
        edge = -(-width // 2)
        count = coarse.layers + 2 * edge
        value = error[coarse.halo - edge : coarse.halo + coarse.layers + edge]
        value = right(value.reshape(count * coarse.ring, coarse.lanes), (b0, b1)[i][...])
        value = left((d0, d1)[i][...], value).reshape(count, fine.ring, fine.lanes)
        for l in range(-width, fine.layers + width):
            new[l + fine.halo] = base[l + fine.halo] + value[l // 2 + edge]

    def residual_into(i, u, target):
        lev = lv[i]

        def body(l):
            target[l - lev.halo] = residual(i, u, l)[1][0 : lev.send_rows]

        loop(lev.halo, lev.halo + lev.layers, body)

    middle = v["k0"].at[pl.ds(l0.halo, l0.layers), pl.ds(0, l0.rows), :]
    middle_s = v["s0"].at[pl.ds(l0.halo, l0.layers), pl.ds(0, l0.rows), :]
    pack(ex["r1"])
    peers = len(far) - 1 + sum(jnp.where(has[dz], len(far), 0) for dz in (1, -1))
    pl.semaphore_wait(barrier, peers)
    send(ex["r1"])
    restrict(0, middle, v["xk1"], 0.125)
    restrict(0, middle_s, v["xs1"], 0.5)
    pack(ex["t1"])
    send(ex["t1"])
    restrict(1, v["xk1"], v["xk2"], 0.125)
    restrict(1, v["xs1"], v["xs2"], 0.5)
    pack(ex["t2"])
    send(ex["t2"])

    receive(ex["r1"])
    tables(0, 1)
    sweep(0, v["ua"], v["ub"], 0)
    pack(ex["r2"])
    send(ex["r2"])
    receive(ex["r2"])
    sweep(0, v["ub"], v["uc"], 0)
    pack(ex["r3"])
    send(ex["r3"])
    receive(ex["r3"])
    residual_into(0, v["uc"], v["res0"])
    restrict(0, v["res0"], v["xf1"], 0.5)
    pack(ex["f1"])
    send(ex["f1"])
    receive(ex["t1"])
    tables(1, 4)
    receive(ex["t2"])
    tables(2, 5)
    receive(ex["f1"])

    def first(i, width):
        lev = lv[i]

        def body(l):
            v["ea" + str(i)][l] = v["w" + str(i)][l] * v["f" + str(i)][l]

        loop(lev.halo - width, lev.halo + lev.layers + width, body)

    first(1, 4)
    sweep(1, v["ea1"], v["eb1"], 3)
    residual_into(1, v["eb1"], v["res1"])
    restrict(1, v["res1"], v["xf2"], 0.5)
    pack(ex["f2"])
    send(ex["f2"])
    receive(ex["f2"])
    first(2, 5)
    sweep(2, v["ea2"], v["eb2"], 4)
    sweep(2, v["eb2"], v["ec2"], 3)
    sweep(2, v["ec2"], v["ed2"], 2)
    add_prolonged(1, v["eb1"], v["ed2"], v["ec1"], 3)
    sweep(1, v["ec1"], v["ed1"], 2)
    sweep(1, v["ed1"], v["ea1"], 1)
    add_prolonged(0, v["uc"], v["ea1"], v["ud"], 2)
    sweep(0, v["ud"], v["ue"], 1)

    def last(l):
        mid, res = residual(0, v["ue"], l)
        out[l - l0.halo] = (mid + v["w0"][l] * res)[0 : l0.rows]

    loop(l0.halo, l0.halo + l0.layers, last)
    for e in ex.values():
        sent(e)


def solution(mesh):
    nblk, nax = mesh.shape["blk"], mesh.shape["ax"]

    def local(guess, rhs, kappa, sigma):
        layers, rows, cols = guess.shape
        lv, ex, scratch = plan(layers, rows, cols)
        mats = [
            halve_cols(lv[0], lv[1]),
            halve_cols(lv[1], lv[2]),
            halve_rows(lv[0], lv[1]),
            halve_rows(lv[1], lv[2]),
            halve_cols(lv[0], lv[1]).T,
            halve_cols(lv[1], lv[2]).T,
            double_rows(lv[0], lv[1], lv[1].layers + 2, 2),
            double_rows(lv[1], lv[2], lv[2].layers + 4, 3),
        ]
        mats = [jnp.asarray(m.astype(np.float32), BF16) for m in mats]
        anywhere = pl.BlockSpec(memory_space=pl.ANY)
        vmem = pl.BlockSpec(memory_space=pltpu.VMEM)
        return pl.pallas_call(
            functools.partial(kernel, lv, ex, list(scratch), nblk, nax),
            out_shape=jax.ShapeDtypeStruct(guess.shape, F32),
            in_specs=[anywhere] * 4 + [vmem] * len(mats),
            out_specs=vmem,
            scratch_shapes=list(scratch.values()),
            compiler_params=pltpu.CompilerParams(
                collective_id=0, has_side_effects=True, vmem_limit_bytes=48 * 2**20
            ),
        )(guess, rhs, kappa, sigma, *mats)

    spec = P("blk", "ax", None)
    return jax.shard_map(local, mesh=mesh, in_specs=(spec,) * 4, out_specs=spec, check_vma=False)
```

time: 475 us -> 62.8 us (0.13)
  local copies, waits for them, and re-layouts: 175 us -> 11.9 us
  starting transfers between devices: 147 us -> 0 us
  other arithmetic: 88.7 us -> 0 us
  waiting for transfers between devices: 61.1 us -> 0 us
  Pallas kernels: 0 us -> 50.3 us
    ppermute x68 -> x0, starting transfers between devices: 147 us -> none  [the longest x34 98.3 us: extended_2(): lax.ppermute(lax.slice_in_dim(block, 0, width, axis=dim), axis, backward)]
    reshape x9 -> x0, local copies, waits for them, and re-layouts: 139 us -> none  [the longest x4 127 us: coarsen(): return field.reshape(a // 2, 2, z // 2, 2, r // 2, 2).mean(axis=(1, 3, 5))]
    ppermute x68 -> x0, waiting for transfers between devices: 61.1 us -> none  [the longest x34 46.9 us: extended_2(): lax.ppermute(lax.slice_in_dim(block, 0, width, axis=dim), axis, backward)]
    reduce_sum x6 -> x0, other arithmetic: 52.7 us -> none  [coarsen(): return field.reshape(a // 2, 2, z // 2, 2, r // 2, 2).mean(axis=(1, 3, 5))]
    pallas_call x0 -> x1, Pallas kernels: none -> 50.3 us  [local(): pl.pallas_call(functools.partial(kernel, lv, ex, list(scratch), nblk, nax...]
    add x14 -> x0, other arithmetic: 14.9 us -> none  [the longest x12 12.4 us: sweep(): return center + omega_factor * resid / diag]
    broadcast_in_dim x13 -> x0, local copies, waits for them, and re-layouts: 11 us -> none  [the longest x6 8.45 us: refine(): return jnp.repeat(jnp.repeat(jnp.repeat(field, 2, 0), 2, 1), 2, 2)]
    unnamed x77 -> x25, local copies, waits for them, and re-layouts: 1.73 us -> 11.9 us
  transfers between devices with their start and end apart: 68 -> 0, of which waited for: 26 -> 0; matrix products, arithmetic and copies ran while one was open for 33% -> 0% of each run, Pallas kernels for 0% -> 0%
where the time goes in v1:
time: 62.8 us; the launch traced here: 62.2 us
  Pallas kernels  50.3 us (80%)
  local copies, waits for them, and re-layouts  11.9 us (19%)
    pallas_call x1, Pallas kernels, local(): pl.pallas_call(functools.partial(kernel, lv, ex, list(scratch), nblk, nax...  50.3 us
    unnamed x25, local copies, waits for them, and re-layouts  11.9 us

profile of v1, /device:TPU:0, one launch (start us, length us, event | category | flops | bytes accessed | tf_op | source)
XLA Modules:
  0.0 62.2 jit_solution(13044477965745000392)
XLA Ops:
  0.0 0.0 copy-start
  0.0 1.1 %copy-done = f32[16,24,384]{2,1,0:T(8,128)S(1)} copy-done((f32[16,24,384]{2,1,0:T(8,128)S(1)}, f32[16,24,384]{2,1,0:T(8,128)}, u32[]{:S(2)}) %copy-start) | copy-done | bytes 589848
  1.1 0.0 copy-start.1
  1.1 1.1 %copy-done.1 = f32[16,24,384]{2,1,0:T(8,128)S(1)} copy-done((f32[16,24,384]{2,1,0:T(8,128)S(1)}, f32[16,24,384]{2,1,0:T(8,128)}, u32[]{:S(2)}) %copy-start.1) | copy-done | bytes 589848
  2.1 0.0 copy-start.2
  2.1 1.1 %copy-done.2 = f32[16,24,384]{2,1,0:T(8,128)S(1)} copy-done((f32[16,24,384]{2,1,0:T(8,128)S(1)}, f32[16,24,384]{2,1,0:T(8,128)}, u32[]{:S(2)}) %copy-start.2) | copy-done | bytes 589848
  3.2 0.0 copy-start.3
  3.2 1.1 %copy-done.3 = f32[16,24,384]{2,1,0:T(8,128)S(1)} copy-done((f32[16,24,384]{2,1,0:T(8,128)S(1)}, f32[16,24,384]{2,1,0:T(8,128)}, u32[]{:S(2)}) %copy-start.3) | copy-done | bytes 589848
  4.3 0.0 copy-start.4
  4.3 0.9 %copy-done.4 = bf16[256,384]{1,0:T(8,128)(2,1)S(1)} copy-done((bf16[256,384]{1,0:T(8,128)(2,1)S(1)}, bf16[256,384]{1,0:T(8,128)(2,1)}, u32[]{:S(2)}) %copy-start.4) | copy-done | bytes 196632
  5.2 0.0 copy-start.5
  5.2 0.9 %copy-done.5 = bf16[384,256]{1,0:T(8,128)(2,1)S(1)} copy-done((bf16[384,256]{1,0:T(8,128)(2,1)S(1)}, bf16[384,256]{1,0:T(8,128)(2,1)}, u32[]{:S(2)}) %copy-start.5) | copy-done | bytes 196632
  6.1 0.0 copy-start.6
  6.1 0.9 %copy-done.6 = bf16[320,240]{1,0:T(8,128)(2,1)S(1)} copy-done((bf16[320,240]{1,0:T(8,128)(2,1)S(1)}, bf16[320,240]{1,0:T(8,128)(2,1)}, u32[]{:S(2)}) %copy-start.6) | copy-done | bytes 153624
  7.0 0.0 copy-start.7
  7.0 0.9 %copy-done.7 = bf16[192,192]{1,0:T(8,128)(2,1)S(1)} copy-done((bf16[192,192]{1,0:T(8,128)(2,1)S(1)}, bf16[192,192]{1,0:T(8,128)(2,1)}, u32[]{:S(2)}) %copy-start.7) | copy-done | bytes 73752
  7.9 0.0 copy-start.8
  7.9 0.8 %copy-done.8 = bf16[128,256]{1,0:T(8,128)(2,1)S(1)} copy-done((bf16[128,256]{1,0:T(8,128)(2,1)S(1)}, bf16[128,256]{1,0:T(8,128)(2,1)}, u32[]{:S(2)}) %copy-start.8) | copy-done | bytes 65560
  8.8 0.0 copy-start.9
  8.8 0.8 %copy-done.9 = bf16[128,192]{1,0:T(8,128)(2,1)S(1)} copy-done((bf16[128,192]{1,0:T(8,128)(2,1)S(1)}, bf16[128,192]{1,0:T(8,128)(2,1)}, u32[]{:S(2)}) %copy-start.9) | copy-done | bytes 49176
  9.6 0.0 copy-start.10
  9.6 0.8 %copy-done.10 = bf16[256,128]{1,0:T(8,128)(2,1)S(1)} copy-done((bf16[256,128]{1,0:T(8,128)(2,1)S(1)}, bf16[256,128]{1,0:T(8,128)(2,1)}, u32[]{:S(2)}) %copy-start.10) | copy-done | bytes 65560
  10.4 0.0 copy-start.11
  10.4 0.7 %copy-done.11 = bf16[32,64]{1,0:T(8,128)(2,1)S(1)} copy-done((bf16[32,64]{1,0:T(8,128)(2,1)S(1)}, bf16[32,64]{1,0:T(8,128)(2,1)}, u32[]{:S(2)}) %copy-start.11) | copy-done | bytes 4120
  11.1 50.3 %shard_map.118 = f32[16,24,384]{2,1,0:T(8,128)S(1)} custom-call(f32[16,24,384]{2,1,0:T(8,128)S(1)} %copy-done, f32[16,24,384]{2,1,0:T(8,128)S(1)} %copy-done.1, f32[16,24,384]{2,1,0:T(8,128)S(1)} %copy-done.2, f32[16,24,384]{2,1,0:T(8,128)S(1)} %copy-done.3, bf16[384,256]{1,0:T(8,128)(2,1)S(1)} %copy-done.5, bf16[256,128]{1,0:T(8,128)(2,1)S(1)} %copy-done.10, ...), custom_call_target="tpu_custom_call" | custom-call | tf_op jit(solution)/shard_map/pallas_call | solution.py:432
  61.4 0.8 %copy.14 = f32[16,24,384]{2,1,0:T(8,128)} copy(f32[16,24,384]{2,1,0:T(8,128)S(1)} %shard_map.118) | data formatting | bytes 1179648
Async XLA Ops:
  0.0 1.1 %copy-start = (f32[16,24,384]{2,1,0:T(8,128)S(1)}, f32[16,24,384]{2,1,0:T(8,128)}, u32[]{:S(2)}) copy-start(f32[16,24,384]{2,1,0:T(8,128)} %refs_0_.1) | copy-start | bytes 1769476
  1.1 1.1 %copy-start.1 = (f32[16,24,384]{2,1,0:T(8,128)S(1)}, f32[16,24,384]{2,1,0:T(8,128)}, u32[]{:S(2)}) copy-start(f32[16,24,384]{2,1,0:T(8,128)} %refs_1_.1) | copy-start | bytes 1769476
  2.1 1.1 %copy-start.2 = (f32[16,24,384]{2,1,0:T(8,128)S(1)}, f32[16,24,384]{2,1,0:T(8,128)}, u32[]{:S(2)}) copy-start(f32[16,24,384]{2,1,0:T(8,128)} %refs_2_.1) | copy-start | bytes 1769476
  3.2 1.1 %copy-start.3 = (f32[16,24,384]{2,1,0:T(8,128)S(1)}, f32[16,24,384]{2,1,0:T(8,128)}, u32[]{:S(2)}) copy-start(f32[16,24,384]{2,1,0:T(8,128)} %refs_3_.1) | copy-start | bytes 1769476
  4.3 0.9 %copy-start.4 = (bf16[256,384]{1,0:T(8,128)(2,1)S(1)}, bf16[256,384]{1,0:T(8,128)(2,1)}, u32[]{:S(2)}) copy-start(bf16[256,384]{1,0:T(8,128)(2,1)} %constant.20.clone.refs_8_) | copy-start | bytes 589828
  5.2 0.9 %copy-start.5 = (bf16[384,256]{1,0:T(8,128)(2,1)S(1)}, bf16[384,256]{1,0:T(8,128)(2,1)}, u32[]{:S(2)}) copy-start(bf16[384,256]{1,0:T(8,128)(2,1)} %constant.16.clone.refs_4_) | copy-start | bytes 589828
  6.1 0.9 %copy-start.6 = (bf16[320,240]{1,0:T(8,128)(2,1)S(1)}, bf16[320,240]{1,0:T(8,128)(2,1)}, u32[]{:S(2)}) copy-start(bf16[320,240]{1,0:T(8,128)(2,1)} %constant.22.clone.refs_10_) | copy-start | bytes 460804
  7.0 0.9 %copy-start.7 = (bf16[192,192]{1,0:T(8,128)(2,1)S(1)}, bf16[192,192]{1,0:T(8,128)(2,1)}, u32[]{:S(2)}) copy-start(bf16[192,192]{1,0:T(8,128)(2,1)} %constant.23.clone.refs_11_) | copy-start | bytes 221188
  7.9 0.8 %copy-start.8 = (bf16[128,256]{1,0:T(8,128)(2,1)S(1)}, bf16[128,256]{1,0:T(8,128)(2,1)}, u32[]{:S(2)}) copy-start(bf16[128,256]{1,0:T(8,128)(2,1)} %constant.21.clone.refs_9_) | copy-start | bytes 196612
  8.8 0.8 %copy-start.9 = (bf16[128,192]{1,0:T(8,128)(2,1)S(1)}, bf16[128,192]{1,0:T(8,128)(2,1)}, u32[]{:S(2)}) copy-start(bf16[128,192]{1,0:T(8,128)(2,1)} %constant.18.clone.refs_6_) | copy-start | bytes 147460
  9.6 0.8 %copy-start.10 = (bf16[256,128]{1,0:T(8,128)(2,1)S(1)}, bf16[256,128]{1,0:T(8,128)(2,1)}, u32[]{:S(2)}) copy-start(bf16[256,128]{1,0:T(8,128)(2,1)} %constant.17.clone.refs_5_) | copy-start | bytes 196612
  10.4 0.7 %copy-start.11 = (bf16[32,64]{1,0:T(8,128)(2,1)S(1)}, bf16[32,64]{1,0:T(8,128)(2,1)}, u32[]{:S(2)}) copy-start(bf16[32,64]{1,0:T(8,128)(2,1)} %constant.19.clone.refs_7_) | copy-start | bytes 12292
